TPU v7x, 32 devices: a whole 2x2x4 slice. The times are simulated.
32 devices in a mesh: owner: 4 (over x, core), shard: 8 (over z, y).
Axes of the slice: x: 2, y: 2, z: 4, core: 2. Of those that a mesh axis runs over, the one named last changes fastest.
Arguments:
- tokens: bfloat16 [96, 7168], P('shard', 'owner'), may hold values from -6 to 6
- expert_ids: int32 [96, 8], P('shard'), may hold values from 0 to 47, all different within a row; in each aligned block of 12 rows (0 to 11, 12 to 23, ...) at most 3 rows name the same one
- gate_weight: bfloat16 [48, 7168, 1024], P('shard', 'owner'), may hold values from -0.0625 to 0.0625
- up_weight: bfloat16 [48, 7168, 1024], P('shard', 'owner'), may hold values from -0.0625 to 0.0625
- trainer_down: float32 [48, 1024, 7168], P('shard', None, 'owner'), may hold values from -0.1875 to 0.1875
Outputs:
- hidden: bfloat16 [24, 48, 1024], P('owner', 'shard')
- new_down: bfloat16 [48, 1024, 7168], P('shard', 'owner')
Inputs may be any that keep to these rules, and one draw needn't show every extreme that they name: `expert_ids`: within the rows of one index of shard (aligned blocks of 12 rows) no expert is named by more than 3 rows, a bound that some block reaches.
All inputs are finite; a program needn't handle non-finite values.
Results may differ from a plain program's by a relative error of at most 0.0017.
Values may be sent and summed in bfloat16 or wider, within the bound.
A program may use at most 256 MiB of HBM per device.

v0:
```python
import jax
import jax.numpy as jnp
from jax import lax
from jax.sharding import PartitionSpec as P

TOP = 8
FF = 1024
EXPERTS = 48
CAP = 3


def on_device(tokens, expert_ids, gate_weight, up_weight, trainer_down):
    rows, width = tokens.shape
    flat = expert_ids.reshape(-1)
    hits = (flat[:, None] == jnp.arange(EXPERTS, dtype=jnp.int32)[None, :]).astype(jnp.int32)
    before = jnp.cumsum(hits, axis=0) - hits
    place = jnp.sum(before * hits, axis=1)
    target = place * EXPERTS + flat
    select = (target[:, None] == jnp.arange(CAP * EXPERTS, dtype=jnp.int32)[None, :]).astype(
        jnp.int32
    )
    select = jnp.sum(select.reshape(rows, TOP, CAP * EXPERTS), axis=1).astype(jnp.bfloat16)
    sent = jnp.einsum("rs,rd->sd", select, tokens, preferred_element_type=jnp.float32)
    sent = sent.astype(jnp.bfloat16).reshape(CAP, EXPERTS, width)
    received = lax.all_to_all(sent, "shard", split_axis=1, concat_axis=0, tiled=True)
    share = received.shape[0] // lax.axis_size("owner")
    gate = jnp.einsum("sed,edf->sef", received, gate_weight, preferred_element_type=jnp.float32)
    up = jnp.einsum("sed,edf->sef", received, up_weight, preferred_element_type=jnp.float32)
    totals = lax.psum(jnp.concatenate([gate, up], axis=2), "owner")
    summed = lax.dynamic_slice_in_dim(totals, lax.axis_index("owner") * share, share, 0)
    gate_sum = summed[:, :, :FF]
    up_sum = summed[:, :, FF:]
    hidden = (jax.nn.silu(gate_sum) * up_sum).astype(jnp.bfloat16)
    new_down = lax.all_to_all(
        trainer_down.astype(jnp.bfloat16), "owner", split_axis=1, concat_axis=2, tiled=True
    )
    return (hidden, new_down)


def solution(mesh):
    in_specs = (
        P("shard", "owner"),
        P("shard", None),
        P("shard", "owner", None),
        P("shard", "owner", None),
        P("shard", None, "owner"),
    )
    out_specs = (P("owner", "shard", None), P("shard", "owner", None))
    return jax.shard_map(
        on_device, mesh=mesh, in_specs=in_specs, out_specs=out_specs, check_vma=False
    )
```

profile of v0, /device:TPU:1, one launch (start us, length us, event | category | flops | bytes accessed | tf_op | source)
XLA Modules:
  0.0 474.6 jit_solution(12478548986101952844)
XLA Ops:
  7.2 0.0 copy-start
  7.2 0.8 copy.33
  8.0 0.1 eq.29
  8.1 0.1 fusion.1
  8.1 0.1 reduce_window_sum.11
  8.3 0.2 select_reduce_fusion
  8.5 0.1 mul.29
  8.6 0.1 convert_reduce_fusion
  8.7 0.0 copy-done
  8.7 0.3 convolution_convert_fusion
  9.0 1.2 copy.35
  10.2 6.4 %all-to-all-start = ((bf16[3,48,1792]{2,0,1:T(4,128)(2,1)}), bf16[3,48,1792]{2,0,1:T(4,128)(2,1)S(1)}, u32[]{:S(2)}, u32[]{:S(2)}) async-start(bf16[3,48,1792]{2,0,1:T(4,128)(2,1)} %copy.35), calls=%async_computation | async-start | bytes 1376256 | tf_op jit(solution)/shard_map/all_to_all | solution.py:25
  16.6 23.5 %convert_element_type.24 = bf16[6,1024,1792]{2,1,0:T(8,128)(2,1)} convert(f32[6,1024,1792]{2,1,0:T(8,128)} %param.9) | non-fusion elementwise | flops 11010048 | bytes 66060288 | tf_op jit(solution)/shard_map/convert_element_type | solution.py:35
  40.1 23.8 %copy.38 = bf16[6,1024,1792]{2,0,1:T(8,128)(2,1)} copy(bf16[6,1024,1792]{2,1,0:T(8,128)(2,1)} %convert_element_type.24) | data formatting | bytes 44040192 | tf_op jit(solution)/shard_map/convert_element_type | solution.py:35
  63.9 0.0 all-to-all-done
  64.0 10.0 %all-to-all-start.1 = ((bf16[6,1024,1792]{2,0,1:T(8,128)(2,1)}), bf16[6,1024,1792]{2,0,1:T(8,128)(2,1)}, u32[]{:S(2)}, u32[]{:S(2)}) async-start(bf16[6,1024,1792]{2,0,1:T(8,128)(2,1)} %copy.38), calls=%async_computation.1 | async-start | bytes 58720256 | tf_op jit(solution)/shard_map/all_to_all | solution.py:34
  74.0 0.0 all-reduce.2.cloned.1.call-start
  74.0 0.1 copy.43
  74.1 0.4 copy.37
  74.5 0.4 all_to_all.29
  74.9 8.8 %convolution_bitcast_fusion = f32[24,6,1024]{2,0,1:T(8,128)S(1)} fusion(bf16[24,6,1792]{2,0,1:T(8,128)(2,1)S(1)} %all_to_all.29, bf16[6,1792,1024]{2,1,0:T(8,128)(2,1)} %param.8), kind=kOutput, calls=%fused_computation.1 | convolution fusion | flops 528482304 | bytes 23126016 | tf_op jit(solution)/shard_map/sed,edf->sef/dot_general | solution.py:28
  83.8 8.8 %convolution_bitcast_fusion.1 = f32[24,6,1024]{2,0,1:T(8,128)S(1)} fusion(bf16[24,6,1792]{2,0,1:T(8,128)(2,1)S(1)} %all_to_all.29, bf16[6,1792,1024]{2,1,0:T(8,128)(2,1)} %param.7), kind=kOutput, calls=%fused_computation.2 | convolution fusion | flops 528482304 | bytes 23126016 | tf_op jit(solution)/shard_map/sed,edf->sef/dot_general | solution.py:27
  92.6 1.1 pad_maximum_fusion
  93.7 0.0 all-reduce.2.cloned.1.call-update
  93.7 57.3 %all-reduce.2.cloned.1.call-done = f32[24,6,2048]{2,0,1:T(8,128)} async-done(((f32[24,6,2048]{2,0,1:T(8,128)}), f32[24,6,2048]{2,0,1:T(8,128)}) %all-reduce.2.cloned.1.call-update) | async-done | bytes 1179664 | tf_op jit(solution)/shard_map/psum | solution.py:29
  151.0 1.2 fusion
  152.3 0.7 copy.40
  153.0 257.0 %all-to-all-done.1 = bf16[6,1024,1792]{2,0,1:T(8,128)(2,1)} async-done(((bf16[6,1024,1792]{2,0,1:T(8,128)(2,1)}), bf16[6,1024,1792]{2,0,1:T(8,128)(2,1)}, u32[]{:S(2)}, u32[]{:S(2)}) %all-to-all-start.1) | async-done | bytes 22020128 | tf_op jit(solution)/shard_map/all_to_all | solution.py:34
  410.0 0.0 copy-start.1
  410.0 20.6 %copy.39 = bf16[6,256,4,1792]{3,2,1,0:T(4,128)(2,1)} copy(bf16[6,256,4,1792]{3,0,1,2:T(8,128)(2,1)} %bitcast.6) | data formatting | bytes 44040192 | tf_op jit(solution)/shard_map/all_to_all | solution.py:34
  430.6 37.2 %all_to_all.33 = bf16[6,256,7168]{2,1,0:T(8,128)(2,1)} reshape(bf16[6,256,4,1792]{3,2,1,0:T(4,128)(2,1)} %copy.39) | data formatting | bytes 44040192 | tf_op jit(solution)/shard_map/all_to_all | solution.py:34
  467.8 0.0 copy-done.1
  (2 shorter events, 0.0 us)
Async XLA Ops:
  7.2 1.5 copy-start
  10.2 53.7 %all-to-all-start = ((bf16[3,48,1792]{2,0,1:T(4,128)(2,1)}), bf16[3,48,1792]{2,0,1:T(4,128)(2,1)S(1)}, u32[]{:S(2)}, u32[]{:S(2)}) async-start(bf16[3,48,1792]{2,0,1:T(4,128)(2,1)} %copy.35), calls=%async_computation | async-start | bytes 1376256 | tf_op jit(solution)/shard_map/all_to_all | solution.py:25
  64.0 346.0 %all-to-all-start.1 = ((bf16[6,1024,1792]{2,0,1:T(8,128)(2,1)}), bf16[6,1024,1792]{2,0,1:T(8,128)(2,1)}, u32[]{:S(2)}, u32[]{:S(2)}) async-start(bf16[6,1024,1792]{2,0,1:T(8,128)(2,1)} %copy.38), calls=%async_computation.1 | async-start | bytes 58720256 | tf_op jit(solution)/shard_map/all_to_all | solution.py:34
  74.0 77.1 %all-reduce.2.cloned.1.call-start = ((), (), s32[]{:S(2)}) async-start(), calls=%async_computation.2 | async-start | bytes 2359296 | tf_op jit(solution)/shard_map/psum | solution.py:29
  410.0 57.8 %copy-start.1 = (bf16[12,1792]{1,0:T(8,128)(2,1)S(1)}, bf16[12,1792]{1,0:T(8,128)(2,1)}, u32[]{:S(2)}) copy-start(bf16[12,1792]{1,0:T(8,128)(2,1)} %param.5) | copy-start | bytes 129028
Sparse Core Ops, SparseCore 0:
  93.9 57.1 all-reduce.1
where the time goes:
time: 477 us; the launch traced here: 475 us
  waiting for transfers between devices  314 us (66%)
  local copies, waits for them, and re-layouts  85.4 us (18%)
  other arithmetic  26.4 us (6%)
  matrix products  18 us (4%)
  starting transfers between devices  16.4 us (3%)
  between operations  14.1 us (3%)
    all_to_all x1, waiting for transfers between devices, on_device(): lax.all_to_all(trainer_down.astype(jnp.bfloat16), 'owner', split_axis=1,...  257 us
    all_to_all x2, local copies, waits for them, and re-layouts, on_device(): lax.all_to_all(trainer_down.astype(jnp.bfloat16), 'owner', split_axis=1,...  57.8 us
    psum x1, waiting for transfers between devices, on_device(): totals = lax.psum(jnp.concatenate([gate, up], axis=2), 'owner')  57.3 us
    convert_element_type x1, local copies, waits for them, and re-layouts, on_device(): trainer_down.astype(jnp.bfloat16)  23.8 us
    convert_element_type x1, other arithmetic, on_device(): trainer_down.astype(jnp.bfloat16)  23.5 us
    all_to_all x1, starting transfers between devices, on_device(): lax.all_to_all(trainer_down.astype(jnp.bfloat16), 'owner', split_axis=1,...  10 us
  transfers between devices with their start and end apart: 3, of which 2 were waited for; matrix products, arithmetic and copies ran while one was open for 14% of the time, Pallas kernels for 0%

commit v1 on v0

v1 whole, which is shorter than its diff:
```python
import functools

import jax
import jax.numpy as jnp
from jax import lax
from jax.experimental import pallas as pl
from jax.experimental.pallas import tpu as pltpu
from jax.sharding import PartitionSpec as P

MESH = pl.DeviceIdType.MESH
CAP = 3
LOADS = 4
WEIGHTS = 3


def pad(x, m):
    return -(-x // m) * m


def owner_at(n, me, dc, dk):
    return lax.rem(me // 2 + dc, n // 2) * 2 + lax.rem(me % 2 + dk, 2)


def kernel(
    n, n_shard, cap, share, share_pad,
    tokens_ref, ids_ref, gate_ref, up_ref, trainer_ref,
    hidden_ref, land_ref,
    rows32, tok_all, ids_all, disp, w_buf, t_buf, send_buf, part, sib, far,
    load_sem, w_sem, own_sem, send_sem, recv_sem,
    tok_send, tok_recv, ids_send, ids_recv, sib_send, sib_recv, far_send, far_recv,
):
    me, me_s = lax.axis_index("owner"), lax.axis_index("shard")
    chips, chip, core = n // 2, me // 2, me % 2
    experts, depth, ff = gate_ref.shape
    rows = trainer_ref.shape[1] // n
    n_rows, top = ids_ref.shape
    pad_rows = tok_all.shape[1]

    far_jobs = [(e, dc, dk) for e in range(experts) for dc in range(1, chips) for dk in (0, 1)]
    near_jobs = [(e, 0, dk) for dk in (1, 0) for e in range(experts)]
    jobs = far_jobs + near_jobs
    early = max(1, len(far_jobs) // 3)

    def load(j):
        e, dc, dk = jobs[j]
        to = owner_at(n, me, dc, dk)
        at = pl.ds(pl.multiple_of(to * rows, rows), rows)
        return pltpu.make_async_copy(
            trainer_ref.at[e, at], t_buf.at[j % LOADS], load_sem.at[j % LOADS]
        )

    def ship(j):
        e, dc, dk = jobs[j]
        if dc == 0 and dk == 0:
            return pltpu.make_async_copy(send_buf.at[j], land_ref.at[e, me], own_sem.at[e])
        return pltpu.make_async_remote_copy(
            src_ref=send_buf.at[j], dst_ref=land_ref.at[e, me],
            send_sem=send_sem.at[j], recv_sem=recv_sem.at[j],
            device_id=(owner_at(n, me, dc, dk), me_s), device_id_type=MESH,
        )

    step = 32 if rows % 32 == 0 else 16

    def run(j):
        load(j).wait()

        def cast(i, _):
            at = pl.ds(pl.multiple_of(i * step, step), step)
            send_buf[j, at] = t_buf[j % LOADS, at].astype(jnp.bfloat16)
            return 0

        lax.fori_loop(0, rows // step, cast, 0)
        if j + LOADS < len(jobs):
            load(j + LOADS).start()
        ship(j).start()

    matrices = [(e, g) for e in range(experts) for g in (0, 1)]

    def weight(i):
        e, g = matrices[i]
        source = (gate_ref, up_ref)[g]
        return pltpu.make_async_copy(source.at[e], w_buf.at[i % WEIGHTS], w_sem.at[i % WEIGHTS])

    for j in range(min(LOADS, len(jobs))):
        load(j).start()

    rows32[...] = jnp.zeros_like(rows32)
    rows32[0:n_rows, :] = tokens_ref[...].astype(jnp.float32)
    tok_all[me_s] = rows32[...].astype(jnp.bfloat16)
    ids_all[me_s] = jnp.full(ids_all.shape[1:], -1, jnp.int32)
    ids_all[me_s, 0:n_rows, 0:top] = ids_ref[...]

    barrier = pltpu.get_barrier_semaphore()
    others = [(dc, dk) for dc in range(chips) for dk in (0, 1) if (dc, dk) != (0, 0)]
    for dc, dk in others:
        pl.semaphore_signal(
            barrier, inc=1, device_id=(owner_at(n, me, dc, dk), me_s), device_id_type=MESH
        )
    for k in range(1, n_shard):
        pl.semaphore_signal(
            barrier, inc=1, device_id=(me, lax.rem(me_s + k, n_shard)), device_id_type=MESH
        )
    pl.semaphore_wait(barrier, n - 1 + n_shard - 1)

    def pass_on(k, ref, sends, recvs):
        return pltpu.make_async_remote_copy(
            src_ref=ref.at[me_s], dst_ref=ref.at[me_s],
            send_sem=sends.at[k], recv_sem=recvs.at[k],
            device_id=(me, lax.rem(me_s + k, n_shard)), device_id_type=MESH,
        )

    token_copies = []
    for k in range(1, n_shard):
        token_copies.append(pass_on(k, tok_all, tok_send, tok_recv))
        token_copies.append(pass_on(k, ids_all, ids_send, ids_recv))
    for copy in token_copies:
        copy.start()

    for j in range(early):
        run(j)
    for i in range(min(WEIGHTS, len(matrices))):
        weight(i).start()
    for copy in token_copies:
        copy.wait()

    all_rows = n_shard * pad_rows
    slots = n * share_pad
    ids = ids_all[...].reshape(all_rows, ids_all.shape[2])
    r = lax.broadcasted_iota(jnp.int32, (all_rows, all_rows), 0)
    q = lax.broadcasted_iota(jnp.int32, (all_rows, all_rows), 1)
    earlier = jnp.where((r // pad_rows == q // pad_rows) & (q < r), 1.0, 0.0).astype(jnp.bfloat16)
    lane = lax.broadcasted_iota(jnp.int32, (all_rows, 128), 1)
    hits = jnp.zeros((all_rows, 128), jnp.float32)
    for k in range(top):
        hits = hits + jnp.where(ids[:, k : k + 1] == me_s * experts + lane, 1.0, 0.0)
    hits = jnp.where(lane < experts, hits, 0.0)
    before = jnp.dot(earlier, hits.astype(jnp.bfloat16), preferred_element_type=jnp.float32)
    before = before.astype(jnp.int32)
    block = lax.broadcasted_iota(jnp.int32, (all_rows, 1), 0) // pad_rows
    place = lax.broadcasted_iota(jnp.int32, (all_rows, slots), 1)
    tokens = tok_all[...].reshape(all_rows, depth)
    for e in range(experts):
        slot = block * cap + before[:, e : e + 1]
        slot = slot // share * share_pad + slot % share
        chosen = jnp.where(place == slot, hits[:, e : e + 1], 0.0).astype(jnp.bfloat16)
        disp[e] = lax.dot_general(
            chosen, tokens, (((0,), (0,)), ((), ())), preferred_element_type=jnp.float32
        ).astype(jnp.bfloat16)

    for i, (e, g) in enumerate(matrices):
        weight(i).wait()
        total = jnp.dot(disp[e], w_buf[i % WEIGHTS], preferred_element_type=jnp.float32)
        for o in range(n):
            part[o, e, g] = total[o * share_pad : (o + 1) * share_pad]
        if i + WEIGHTS < len(matrices):
            weight(i + WEIGHTS).start()

    def to_sibling(c):
        return pltpu.make_async_remote_copy(
            src_ref=part.at[c * 2 + 1 - core], dst_ref=sib.at[c],
            send_sem=sib_send.at[c], recv_sem=sib_recv.at[c],
            device_id=(owner_at(n, me, 0, 1), me_s), device_id_type=MESH,
        )

    def to_chip(dc):
        c = lax.rem(chip + dc, chips)
        return pltpu.make_async_remote_copy(
            src_ref=part.at[c * 2 + core], dst_ref=far.at[dc],
            send_sem=far_send.at[dc], recv_sem=far_recv.at[dc],
            device_id=(owner_at(n, me, dc, 0), me_s), device_id_type=MESH,
        )

    for c in range(chips):
        to_sibling(c).start()
    for c in range(chips):
        to_sibling(c).wait()
    for c in range(chips):
        part[c * 2 + core] = part[c * 2 + core] + sib[c]
    for dc in range(1, chips):
        to_chip(dc).start()

    for j in range(early, len(jobs)):
        run(j)

    for dc in range(1, chips):
        to_chip(dc).wait()
    for e in range(experts):
        gate, up = part[me, e, 0], part[me, e, 1]
        for dc in range(1, chips):
            gate, up = gate + far[dc, e, 0], up + far[dc, e, 1]
        hidden_ref[e] = gate / (1.0 + jnp.exp(-gate)) * up

    for j in range(len(jobs)):
        ship(j).wait()


def exchange(tokens, expert_ids, gate_weight, up_weight, trainer_down):
    n, n_shard = lax.axis_size("owner"), lax.axis_size("shard")
    experts, depth, ff = gate_weight.shape
    width, rows = trainer_down.shape[2], trainer_down.shape[1] // n
    n_rows, top = expert_ids.shape
    share = CAP * n_shard // n
    share_pad = pad(share, 8)
    pad_rows = pad(n_rows, 16)
    count = experts * n
    dma = pltpu.SemaphoreType.DMA
    whole = pl.BlockSpec(memory_space=pltpu.VMEM)
    remote = pl.BlockSpec(memory_space=pl.ANY)
    return pl.pallas_call(
        functools.partial(kernel, n, n_shard, CAP, share, share_pad),
        out_shape=(
            jax.ShapeDtypeStruct((experts, share_pad, ff), jnp.float32),
            jax.ShapeDtypeStruct((experts, n, rows, width), jnp.bfloat16),
        ),
        in_specs=[whole, whole, remote, remote, remote],
        out_specs=(whole, remote),
        scratch_shapes=[
            pltpu.VMEM((pad_rows, depth), jnp.float32),
            pltpu.VMEM((n_shard, pad_rows, depth), jnp.bfloat16),
            pltpu.VMEM((n_shard, pad_rows, 128), jnp.int32),
            pltpu.VMEM((experts, n * share_pad, depth), jnp.bfloat16),
            pltpu.VMEM((WEIGHTS, depth, ff), jnp.bfloat16),
            pltpu.VMEM((LOADS, rows, width), jnp.float32),
            pltpu.VMEM((count, rows, width), jnp.bfloat16),
            pltpu.VMEM((n, experts, 2, share_pad, ff), jnp.float32),
            pltpu.VMEM((n // 2, experts, 2, share_pad, ff), jnp.float32),
            pltpu.VMEM((n // 2, experts, 2, share_pad, ff), jnp.float32),
            dma((LOADS,)), dma((WEIGHTS,)), dma((experts,)), dma((count,)), dma((count,)),
            dma((n_shard,)), dma((n_shard,)), dma((n_shard,)), dma((n_shard,)),
            dma((n // 2,)), dma((n // 2,)), dma((n // 2,)), dma((n // 2,)),
        ],
        compiler_params=pltpu.CompilerParams(
            collective_id=0, has_side_effects=True, vmem_limit_bytes=56 * 2**20
        ),
        cost_estimate=pl.CostEstimate(
            flops=4 * experts * n * share_pad * depth * ff,
            bytes_accessed=4 * experts * depth * ff + 6 * experts * n * rows * width,
            transcendentals=experts * share_pad * ff,
        ),
        name="exchange",
    )(tokens, expert_ids, gate_weight, up_weight, trainer_down)


def place_body(x_ref, o_ref):
    o_ref[0] = x_ref[0, 0]


def lay_out(landed):
    experts, n, rows, width = landed.shape
    if width % 128:
        return landed.transpose(0, 2, 1, 3).reshape(experts, rows, n * width)
    return pl.pallas_call(
        place_body,
        grid=(experts, n),
        in_specs=[pl.BlockSpec((1, 1, rows, width), lambda e, o: (e, o, 0, 0))],
        out_specs=pl.BlockSpec((1, rows, width), lambda e, o: (e, 0, o)),
        out_shape=jax.ShapeDtypeStruct((experts, rows, n * width), landed.dtype),
        compiler_params=pltpu.CompilerParams(vmem_limit_bytes=56 * 2**20),
        cost_estimate=pl.CostEstimate(
            flops=0, bytes_accessed=4 * landed.size, transcendentals=0
        ),
        name="lay_out",
    )(landed)


def on_device(tokens, expert_ids, gate_weight, up_weight, trainer_down):
    share = CAP * lax.axis_size("shard") // lax.axis_size("owner")
    hidden, landed = exchange(tokens, expert_ids, gate_weight, up_weight, trainer_down)
    hidden = jnp.swapaxes(hidden[:, :share], 0, 1).astype(jnp.bfloat16)
    return (hidden, lay_out(landed))


def solution(mesh):
    in_specs = (
        P("shard", "owner"),
        P("shard", None),
        P("shard", "owner", None),
        P("shard", "owner", None),
        P("shard", None, "owner"),
    )
    out_specs = (P("owner", "shard", None), P("shard", "owner", None))
    return jax.shard_map(
        on_device, mesh=mesh, in_specs=in_specs, out_specs=out_specs, check_vma=False
    )
```

time: 477 us -> 283 us (0.59)
  waiting for transfers between devices: 314 us -> 0 us
  Pallas kernels: 0 us -> 278 us
  local copies, waits for them, and re-layouts: 85.4 us -> 2.99 us
  other arithmetic: 26.4 us -> 0 us
  matrix products: 18 us -> 0 us
  starting transfers between devices: 16.4 us -> 0 us
  between operations: 14.1 us -> 0.64 us
    pallas_call x0 -> x2, Pallas kernels: none -> 278 us  [the longest x1 254 us: exchange(): pl.pallas_call(functools.partial(kernel, n, n_shard, CAP, share, share_pa...]
    all_to_all x2 -> x0, waiting for transfers between devices: 257 us -> none  [the longest x1 257 us: on_device(): lax.all_to_all(trainer_down.astype(jnp.bfloat16), 'owner', split_axis=1,...]
    all_to_all x5 -> x0, local copies, waits for them, and re-layouts: 58.8 us -> none  [the longest x2 57.8 us: on_device(): lax.all_to_all(trainer_down.astype(jnp.bfloat16), 'owner', split_axis=1,...]
    psum x1 -> x0, waiting for transfers between devices: 57.3 us -> none  [on_device(): totals = lax.psum(jnp.concatenate([gate, up], axis=2), 'owner')]
    convert_element_type x3 -> x0, other arithmetic: 24.8 us -> none  [the longest x1 23.5 us: on_device(): trainer_down.astype(jnp.bfloat16)]
    convert_element_type x1, local copies, waits for them, and re-layouts: 23.8 us -> 0.94 us  [on_device(): hidden = jnp.swapaxes(hidden[:, :share], 0, 1).astype(jnp.bfloat16)]
    dot_general x3 -> x0, matrix products: 18 us -> none  [the longest x1 8.82 us: on_device(): jnp.einsum('sed,edf->sef', received, up_weight, preferred_element_type=jn...]
    all_to_all x2 -> x0, starting transfers between devices: 16.4 us -> none  [the longest x1 10 us: on_device(): lax.all_to_all(trainer_down.astype(jnp.bfloat16), 'owner', split_axis=1,...]
  transfers between devices with their start and end apart: 3 -> 0, of which waited for: 2 -> 0; matrix products, arithmetic and copies ran while one was open for 14% -> 0% of each run, Pallas kernels for 0% -> 0%
where the time goes in v1:
time: 283 us; the launch traced here: 282 us
  Pallas kernels  278 us (98%)
  local copies, waits for them, and re-layouts  2.99 us (1%)
    pallas_call x1, Pallas kernels, exchange(): pl.pallas_call(functools.partial(kernel, n, n_shard, CAP, share, share_pa...  254 us
    pallas_call x1, Pallas kernels, lay_out(): pl.pallas_call(place_body, grid=(experts, n), in_specs=[pl.BlockSpec((1,...  24.1 us

profile of v1, /device:TPU:1, one launch (start us, length us, event | category | flops | bytes accessed | tf_op | source)
XLA Modules:
  0.0 282.0 jit_solution(6551530975668965606)
XLA Ops:
  0.6 1.4 copy.7.ids_ref
  2.0 254.4 %exchange.1 = (f32[6,8,1024]{2,1,0:T(8,128)}, bf16[6,4,256,1792]{3,2,1,0:T(8,128)(2,1)}) custom-call(bf16[12,1792]{1,0:T(8,128)(2,1)} %tokens_ref.1, s32[12,8]{1,0:T(8,128)} %copy.7.ids_ref, bf16[6,1792,1024]{2,1,0:T(8,128)(2,1)} %gate_ref.1, bf16[6,1792,1024]{2,1,0:T(8,128)(2,1)} %up_ref.1, f32[6,1024,1792]{2,1,0:T(8,128)} %trainer_ref.1), custom_call_target="tpu_custom_call" | custom-call | flops 1409286144 | bytes 110100480 | tf_op jit(solution)/shard_map/exchange/pallas_call | solution.py:209
  256.4 0.9 fusion
  257.3 0.7 copy.8
  258.0 24.1 %lay_out.1 = bf16[6,256,7168]{2,1,0:T(8,128)(2,1)} custom-call(bf16[6,4,256,1792]{3,2,1,0:T(8,128)(2,1)} %get-tuple-element.5.x_ref), custom_call_target="tpu_custom_call" | custom-call | bytes 44040192 | tf_op jit(solution)/shard_map/lay_out/pallas_call | solution.py:252

commit v2 on v1

--- a/solution.py
+++ b/solution.py
@@ -33,7 +33,8 @@
     chips, chip, core = n // 2, me // 2, me % 2
     experts, depth, ff = gate_ref.shape
     rows = trainer_ref.shape[1] // n
-    n_rows, top = ids_ref.shape
+    top, n_rows = ids_ref.shape
+    pairs = share * 2
     pad_rows = tok_all.shape[1]
 
     far_jobs = [(e, dc, dk) for e in range(experts) for dc in range(1, chips) for dk in (0, 1)]
@@ -88,7 +89,7 @@
     rows32[0:n_rows, :] = tokens_ref[...].astype(jnp.float32)
     tok_all[me_s] = rows32[...].astype(jnp.bfloat16)
     ids_all[me_s] = jnp.full(ids_all.shape[1:], -1, jnp.int32)
-    ids_all[me_s, 0:n_rows, 0:top] = ids_ref[...]
+    ids_all[me_s, 0:n_rows, 0:top] = ids_ref[...].T
 
     barrier = pltpu.get_barrier_semaphore()
     others = [(dc, dk) for dc in range(chips) for dk in (0, 1) if (dc, dk) != (0, 0)]
@@ -113,10 +114,11 @@
     for k in range(1, n_shard):
         token_copies.append(pass_on(k, tok_all, tok_send, tok_recv))
         token_copies.append(pass_on(k, ids_all, ids_send, ids_recv))
+    run(0)
     for copy in token_copies:
         copy.start()
 
-    for j in range(early):
+    for j in range(1, early):
         run(j)
     for i in range(min(WEIGHTS, len(matrices))):
         weight(i).start()
@@ -151,7 +153,8 @@
         weight(i).wait()
         total = jnp.dot(disp[e], w_buf[i % WEIGHTS], preferred_element_type=jnp.float32)
         for o in range(n):
-            part[o, e, g] = total[o * share_pad : (o + 1) * share_pad]
+            at = e * pairs + g * share
+            part[o, at : at + share] = total[o * share_pad : o * share_pad + share]
         if i + WEIGHTS < len(matrices):
             weight(i + WEIGHTS).start()
 
@@ -185,10 +188,14 @@
     for dc in range(1, chips):
         to_chip(dc).wait()
     for e in range(experts):
-        gate, up = part[me, e, 0], part[me, e, 1]
+        at = e * pairs
+        both = part[me, at : at + pairs]
         for dc in range(1, chips):
-            gate, up = gate + far[dc, e, 0], up + far[dc, e, 1]
-        hidden_ref[e] = gate / (1.0 + jnp.exp(-gate)) * up
+            both = both + far[dc, at : at + pairs]
+        gate, up = both[:share], both[share:]
+        value = gate / (1.0 + jnp.exp(-gate)) * up
+        for s in range(share):
+            hidden_ref[s, e : e + 1] = value[s : s + 1]
 
     for j in range(len(jobs)):
         ship(j).wait()
@@ -203,13 +210,14 @@
     share_pad = pad(share, 8)
     pad_rows = pad(n_rows, 16)
     count = experts * n
+    sums = pad(experts * 2 * share, 8)
     dma = pltpu.SemaphoreType.DMA
     whole = pl.BlockSpec(memory_space=pltpu.VMEM)
     remote = pl.BlockSpec(memory_space=pl.ANY)
     return pl.pallas_call(
         functools.partial(kernel, n, n_shard, CAP, share, share_pad),
         out_shape=(
-            jax.ShapeDtypeStruct((experts, share_pad, ff), jnp.float32),
+            jax.ShapeDtypeStruct((share, experts, ff), jnp.float32),
             jax.ShapeDtypeStruct((experts, n, rows, width), jnp.bfloat16),
         ),
         in_specs=[whole, whole, remote, remote, remote],
@@ -222,9 +230,9 @@
             pltpu.VMEM((WEIGHTS, depth, ff), jnp.bfloat16),
             pltpu.VMEM((LOADS, rows, width), jnp.float32),
             pltpu.VMEM((count, rows, width), jnp.bfloat16),
-            pltpu.VMEM((n, experts, 2, share_pad, ff), jnp.float32),
-            pltpu.VMEM((n // 2, experts, 2, share_pad, ff), jnp.float32),
-            pltpu.VMEM((n // 2, experts, 2, share_pad, ff), jnp.float32),
+            pltpu.VMEM((n, sums, ff), jnp.float32),
+            pltpu.VMEM((n // 2, sums, ff), jnp.float32),
+            pltpu.VMEM((n // 2, sums, ff), jnp.float32),
             dma((LOADS,)), dma((WEIGHTS,)), dma((experts,)), dma((count,)), dma((count,)),
             dma((n_shard,)), dma((n_shard,)), dma((n_shard,)), dma((n_shard,)),
             dma((n // 2,)), dma((n // 2,)), dma((n // 2,)), dma((n // 2,)),
@@ -238,36 +246,61 @@
             transcendentals=experts * share_pad * ff,
         ),
         name="exchange",
-    )(tokens, expert_ids, gate_weight, up_weight, trainer_down)
-
-
-def place_body(x_ref, o_ref):
-    o_ref[0] = x_ref[0, 0]
-
-
-def lay_out(landed):
+    )(tokens, expert_ids.T, gate_weight, up_weight, trainer_down)
+
+
+def place_body(landed_ref, value_ref, out_ref, hidden_ref, buf, in_sem, out_sem):
+    experts, n, rows, width = landed_ref.shape
+    blocks = [(e, o) for e in range(experts) for o in range(n)]
+
+    def fetch(e, o):
+        return pltpu.make_async_copy(landed_ref.at[e, o], buf.at[e, o], in_sem.at[e, o])
+
+    def store(e, o):
+        to = out_ref.at[e, :, pl.ds(o * width, width)]
+        return pltpu.make_async_copy(buf.at[e, o], to, out_sem.at[e, o])
+
+    for e, o in blocks:
+        fetch(e, o).start()
+    hidden_ref[...] = value_ref[...].astype(hidden_ref.dtype)
+    for e, o in blocks:
+        fetch(e, o).wait()
+        store(e, o).start()
+    for e, o in blocks:
+        store(e, o).wait()
+
+
+def lay_out(landed, value):
     experts, n, rows, width = landed.shape
     if width % 128:
-        return landed.transpose(0, 2, 1, 3).reshape(experts, rows, n * width)
-    return pl.pallas_call(
+        landed = landed.transpose(0, 2, 1, 3).reshape(experts, rows, n * width)
+        return value.astype(landed.dtype), landed
+    whole = pl.BlockSpec(memory_space=pltpu.VMEM)
+    remote = pl.BlockSpec(memory_space=pl.ANY)
+    out, hidden = pl.pallas_call(
         place_body,
-        grid=(experts, n),
-        in_specs=[pl.BlockSpec((1, 1, rows, width), lambda e, o: (e, o, 0, 0))],
-        out_specs=pl.BlockSpec((1, rows, width), lambda e, o: (e, 0, o)),
-        out_shape=jax.ShapeDtypeStruct((experts, rows, n * width), landed.dtype),
+        in_specs=[remote, whole],
+        out_specs=(remote, whole),
+        out_shape=(
+            jax.ShapeDtypeStruct((experts, rows, n * width), landed.dtype),
+            jax.ShapeDtypeStruct(value.shape, landed.dtype),
+        ),
+        scratch_shapes=[
+            pltpu.VMEM(landed.shape, landed.dtype),
+            pltpu.SemaphoreType.DMA((experts, n)), pltpu.SemaphoreType.DMA((experts, n)),
+        ],
         compiler_params=pltpu.CompilerParams(vmem_limit_bytes=56 * 2**20),
         cost_estimate=pl.CostEstimate(
             flops=0, bytes_accessed=4 * landed.size, transcendentals=0
         ),
         name="lay_out",
-    )(landed)
+    )(landed, value)
+    return hidden, out
 
 
 def on_device(tokens, expert_ids, gate_weight, up_weight, trainer_down):
-    share = CAP * lax.axis_size("shard") // lax.axis_size("owner")
-    hidden, landed = exchange(tokens, expert_ids, gate_weight, up_weight, trainer_down)
-    hidden = jnp.swapaxes(hidden[:, :share], 0, 1).astype(jnp.bfloat16)
-    return (hidden, lay_out(landed))
+    value, landed = exchange(tokens, expert_ids, gate_weight, up_weight, trainer_down)
+    return lay_out(landed, value)
 
 
 def solution(mesh):

time: 283 us -> 270 us (0.954)
  Pallas kernels: 278 us -> 269 us
  local copies, waits for them, and re-layouts: 2.99 us -> 0 us
    pallas_call x1, Pallas kernels: 24.1 us -> 16.9 us  [lay_out(): pl.pallas_call(place_body, in_specs=[remote, whole], out_specs=(remote, w...]
where the time goes in v2:
time: 270 us
  Pallas kernels  269 us (100%)
    pallas_call x1, Pallas kernels, exchange(): pl.pallas_call(functools.partial(kernel, n, n_shard, CAP, share, share_pa...  252 us
    pallas_call x1, Pallas kernels, lay_out(): pl.pallas_call(place_body, in_specs=[remote, whole], out_specs=(remote, w...  16.9 us

profile of v2, /device:TPU:1, one launch (start us, length us, event | category | flops | bytes accessed | tf_op | source)
XLA Modules:
  0.0 269.8 jit_solution(6701831346103128403)
XLA Ops:
  0.6 252.3 %exchange.1 = (f32[6,6,1024]{2,1,0:T(8,128)}, bf16[6,4,256,1792]{3,2,1,0:T(8,128)(2,1)}) custom-call(bf16[12,1792]{1,0:T(8,128)(2,1)} %tokens_ref.1, s32[8,12]{1,0:T(8,128)} %bitcast.1, bf16[6,1792,1024]{2,1,0:T(8,128)(2,1)} %gate_ref.1, bf16[6,1792,1024]{2,1,0:T(8,128)(2,1)} %up_ref.1, f32[6,1024,1792]{2,1,0:T(8,128)} %trainer_ref.1), custom_call_target="tpu_custom_call" | custom-call | flops 1409286144 | bytes 110100480 | tf_op jit(solution)/shard_map/exchange/pallas_call | solution.py:217
  252.9 16.9 %lay_out.1 = (bf16[6,256,7168]{2,1,0:T(8,128)(2,1)}, bf16[6,6,1024]{2,1,0:T(8,128)(2,1)}) custom-call(bf16[6,4,256,1792]{3,2,1,0:T(8,128)(2,1)} %get-tuple-element.6.landed_ref, f32[6,6,1024]{2,1,0:T(8,128)} %get-tuple-element.7.value_ref), custom_call_target="tpu_custom_call" | custom-call | bytes 44040192 | tf_op jit(solution)/shard_map/lay_out/pallas_call | solution.py:280

commit v3 on v2

--- a/solution.py
+++ b/solution.py
@@ -10,7 +10,7 @@
 MESH = pl.DeviceIdType.MESH
 CAP = 3
 LOADS = 4
-WEIGHTS = 3
+WEIGHTS = 2
 
 
 def pad(x, m):
@@ -26,7 +26,7 @@
     tokens_ref, ids_ref, gate_ref, up_ref, trainer_ref,
     hidden_ref, land_ref,
     rows32, tok_all, ids_all, disp, w_buf, t_buf, send_buf, part, sib, far,
-    load_sem, w_sem, own_sem, send_sem, recv_sem,
+    load_sem, w_sem, send_sem, recv_sem,
     tok_send, tok_recv, ids_send, ids_recv, sib_send, sib_recv, far_send, far_recv,
 ):
     me, me_s = lax.axis_index("owner"), lax.axis_index("shard")
@@ -52,8 +52,6 @@
 
     def ship(j):
         e, dc, dk = jobs[j]
-        if dc == 0 and dk == 0:
-            return pltpu.make_async_copy(send_buf.at[j], land_ref.at[e, me], own_sem.at[e])
         return pltpu.make_async_remote_copy(
             src_ref=send_buf.at[j], dst_ref=land_ref.at[e, me],
             send_sem=send_sem.at[j], recv_sem=recv_sem.at[j],
@@ -64,16 +62,23 @@
 
     def run(j):
         load(j).wait()
+        e, dc, dk = jobs[j]
+        own = dc == 0 and dk == 0
 
         def cast(i, _):
             at = pl.ds(pl.multiple_of(i * step, step), step)
-            send_buf[j, at] = t_buf[j % LOADS, at].astype(jnp.bfloat16)
+            block = t_buf[j % LOADS, at].astype(jnp.bfloat16)
+            if own:
+                land_ref[e, me, at] = block
+            else:
+                send_buf[j, at] = block
             return 0
 
         lax.fori_loop(0, rows // step, cast, 0)
         if j + LOADS < len(jobs):
             load(j + LOADS).start()
-        ship(j).start()
+        if not own:
+            ship(j).start()
 
     matrices = [(e, g) for e in range(experts) for g in (0, 1)]
 
@@ -197,7 +202,7 @@
         for s in range(share):
             hidden_ref[s, e : e + 1] = value[s : s + 1]
 
-    for j in range(len(jobs)):
+    for j in range(len(jobs) - experts):
         ship(j).wait()
 
 
@@ -209,7 +214,7 @@
     share = CAP * n_shard // n
     share_pad = pad(share, 8)
     pad_rows = pad(n_rows, 16)
-    count = experts * n
+    count = experts * (n - 1)
     sums = pad(experts * 2 * share, 8)
     dma = pltpu.SemaphoreType.DMA
     whole = pl.BlockSpec(memory_space=pltpu.VMEM)
@@ -217,11 +222,11 @@
     return pl.pallas_call(
         functools.partial(kernel, n, n_shard, CAP, share, share_pad),
         out_shape=(
-            jax.ShapeDtypeStruct((share, experts, ff), jnp.float32),
-            jax.ShapeDtypeStruct((experts, n, rows, width), jnp.bfloat16),
+            pltpu.VMEM((share, experts, ff), jnp.float32),
+            pltpu.VMEM((experts, n, rows, width), jnp.bfloat16),
         ),
         in_specs=[whole, whole, remote, remote, remote],
-        out_specs=(whole, remote),
+        out_specs=(whole, whole),
         scratch_shapes=[
             pltpu.VMEM((pad_rows, depth), jnp.float32),
             pltpu.VMEM((n_shard, pad_rows, depth), jnp.bfloat16),
@@ -233,39 +238,33 @@
             pltpu.VMEM((n, sums, ff), jnp.float32),
             pltpu.VMEM((n // 2, sums, ff), jnp.float32),
             pltpu.VMEM((n // 2, sums, ff), jnp.float32),
-            dma((LOADS,)), dma((WEIGHTS,)), dma((experts,)), dma((count,)), dma((count,)),
+            dma((LOADS,)), dma((WEIGHTS,)), dma((count,)), dma((count,)),
             dma((n_shard,)), dma((n_shard,)), dma((n_shard,)), dma((n_shard,)),
             dma((n // 2,)), dma((n // 2,)), dma((n // 2,)), dma((n // 2,)),
         ],
         compiler_params=pltpu.CompilerParams(
-            collective_id=0, has_side_effects=True, vmem_limit_bytes=56 * 2**20
+            collective_id=0, has_side_effects=True, vmem_limit_bytes=38 * 2**20
         ),
         cost_estimate=pl.CostEstimate(
             flops=4 * experts * n * share_pad * depth * ff,
-            bytes_accessed=4 * experts * depth * ff + 6 * experts * n * rows * width,
+            bytes_accessed=4 * experts * depth * ff + 4 * experts * n * rows * width,
             transcendentals=experts * share_pad * ff,
         ),
         name="exchange",
     )(tokens, expert_ids.T, gate_weight, up_weight, trainer_down)
 
 
-def place_body(landed_ref, value_ref, out_ref, hidden_ref, buf, in_sem, out_sem):
+def place_body(landed_ref, value_ref, out_ref, hidden_ref, out_sem):
     experts, n, rows, width = landed_ref.shape
     blocks = [(e, o) for e in range(experts) for o in range(n)]
 
-    def fetch(e, o):
-        return pltpu.make_async_copy(landed_ref.at[e, o], buf.at[e, o], in_sem.at[e, o])
-
     def store(e, o):
         to = out_ref.at[e, :, pl.ds(o * width, width)]
-        return pltpu.make_async_copy(buf.at[e, o], to, out_sem.at[e, o])
+        return pltpu.make_async_copy(landed_ref.at[e, o], to, out_sem.at[e, o])
 
     for e, o in blocks:
-        fetch(e, o).start()
+        store(e, o).start()
     hidden_ref[...] = value_ref[...].astype(hidden_ref.dtype)
-    for e, o in blocks:
-        fetch(e, o).wait()
-        store(e, o).start()
     for e, o in blocks:
         store(e, o).wait()
 
@@ -279,19 +278,16 @@
     remote = pl.BlockSpec(memory_space=pl.ANY)
     out, hidden = pl.pallas_call(
         place_body,
-        in_specs=[remote, whole],
+        in_specs=[whole, whole],
         out_specs=(remote, whole),
         out_shape=(
             jax.ShapeDtypeStruct((experts, rows, n * width), landed.dtype),
             jax.ShapeDtypeStruct(value.shape, landed.dtype),
         ),
-        scratch_shapes=[
-            pltpu.VMEM(landed.shape, landed.dtype),
-            pltpu.SemaphoreType.DMA((experts, n)), pltpu.SemaphoreType.DMA((experts, n)),
-        ],
-        compiler_params=pltpu.CompilerParams(vmem_limit_bytes=56 * 2**20),
+        scratch_shapes=[pltpu.SemaphoreType.DMA((experts, n))],
+        compiler_params=pltpu.CompilerParams(vmem_limit_bytes=32 * 2**20),
         cost_estimate=pl.CostEstimate(
-            flops=0, bytes_accessed=4 * landed.size, transcendentals=0
+            flops=0, bytes_accessed=2 * landed.size, transcendentals=0
         ),
         name="lay_out",
     )(landed, value)

time: 270 us -> 261 us (0.967)
  Pallas kernels: 269 us -> 260 us
    pallas_call x1, Pallas kernels: 16.9 us -> 8.25 us  [lay_out(): pl.pallas_call(place_body, in_specs=[whole, whole], out_specs=(remote, wh...]
where the time goes in v3:
time: 261 us; the launch traced here: 260 us
  Pallas kernels  260 us (100%)
    pallas_call x1, Pallas kernels, exchange(): pl.pallas_call(functools.partial(kernel, n, n_shard, CAP, share, share_pa...  251 us
    pallas_call x1, Pallas kernels, lay_out(): pl.pallas_call(place_body, in_specs=[whole, whole], out_specs=(remote, wh...  8.25 us

profile of v3, /device:TPU:1, one launch (start us, length us, event | category | flops | bytes accessed | tf_op | source)
XLA Modules:
  0.0 260.2 jit_solution(6554237082829799391)
XLA Ops:
  0.6 251.3 %exchange.1 = (f32[6,6,1024]{2,1,0:T(8,128)S(1)}, bf16[6,4,256,1792]{3,2,1,0:T(8,128)(2,1)S(1)}) custom-call(bf16[12,1792]{1,0:T(8,128)(2,1)} %tokens_ref.1, s32[8,12]{1,0:T(8,128)} %bitcast.1, bf16[6,1792,1024]{2,1,0:T(8,128)(2,1)} %gate_ref.1, bf16[6,1792,1024]{2,1,0:T(8,128)(2,1)} %up_ref.1, f32[6,1024,1792]{2,1,0:T(8,128)} %trainer_ref.1), custom_call_target="tpu_custom_call" | custom-call | flops 1409286144 | bytes 88080384 | tf_op jit(solution)/shard_map/exchange/pallas_call | solution.py:222
  252.0 8.3 %lay_out.1 = (bf16[6,256,7168]{2,1,0:T(8,128)(2,1)}, bf16[6,6,1024]{2,1,0:T(8,128)(2,1)}) custom-call(bf16[6,4,256,1792]{3,2,1,0:T(8,128)(2,1)S(1)} %get-tuple-element.6.landed_ref, f32[6,6,1024]{2,1,0:T(8,128)S(1)} %get-tuple-element.7.value_ref), custom_call_target="tpu_custom_call" | custom-call | bytes 22020096 | tf_op jit(solution)/shard_map/lay_out/pallas_call | solution.py:279
